TPU v7x, 32 devices: a whole 2x2x4 slice. The times are simulated.
32 devices in a mesh: seq: 8 (over z, x), head: 4 (over y, core).
Axes of the slice: x: 2, y: 2, z: 4, core: 2. Of those that a mesh axis runs over, the one named last changes fastest.
Arguments:
- queries: bfloat16 [2048, 2048], P('seq', 'head'), may hold values from -180 to 180
- keys: bfloat16 [2048, 2048], P('seq', 'head'), may hold values from -7 to 7
- values: bfloat16 [2048, 2048], P('seq', 'head'), may hold values from -6 to 6
- out_grad: bfloat16 [2048, 2048], P('seq', 'head'), may hold values from -6 to 6
- rand_blocks: int32 [32, 3], replicated, may hold values from 0 to 31, as said below
- glob_blocks: int32 [8], P('seq'), may hold values from 0 to 31, as said below
Outputs:
- attn_out: bfloat16 [2048, 2048], P('seq', 'head')
- query_grad: bfloat16 [2048, 2048], P('seq', 'head')
- key_grad: bfloat16 [2048, 2048], P('seq', 'head')
- value_grad: bfloat16 [2048, 2048], P('seq', 'head')
Inputs may be any that keep to these rules, and one draw needn't show every extreme that they name: `rand_blocks`: rows 4 * i to 4 * (i + 1) - 1 are the query blocks of index i of seq. Among their 12 entries, the blocks of any one index j of seq (blocks 4 * j to 4 * (j + 1) - 1) are named at most 2 times; in every draw one index j is named exactly 2 times by the rows of every index i. `glob_blocks`: entry j is one of the blocks 4 * j to 4 * (j + 1) - 1.
All inputs are finite; a program needn't handle non-finite values.
Results may differ from a plain program's by a relative error of at most 0.0052.
Values may be sent and summed in bfloat16 or wider, within the bound.
A program may use at most 128 MiB of HBM per device.

v0:
```python
import math
import jax
import jax.numpy as jnp
from jax import lax
from jax.sharding import PartitionSpec as P

HDIM = 128
BLK = 64
GLEN = 16


def extended(array, sides, width):
    for axis, dim in sides:
        size, length = (lax.axis_size(axis), array.shape[dim])
        up = [(i, (i + 1) % size) for i in range(size - 1)]
        down = [(j, i) for i, j in up]
        last = lax.slice_in_dim(array, length - width, length, axis=dim)
        first = lax.slice_in_dim(array, 0, width, axis=dim)
        before = lax.ppermute(last, axis, up)
        after = lax.ppermute(first, axis, down)
        array = jnp.concatenate([before, array, after], axis=dim)
    return array


def shards(queries, keys, values, out_grad, rand_blocks, glob_blocks):
    rows_dev, width_dev = queries.shape
    head_count = width_dev // HDIM
    seq_count = lax.axis_size("seq")
    my_index = lax.axis_index("seq")
    blocks_dev = rows_dev // BLK
    total_blocks = blocks_dev * seq_count
    per_block = rand_blocks.shape[1]
    spots = blocks_dev * per_block
    capacity = max(2, (spots + seq_count - 1) // seq_count)
    scale = 1.0 / math.sqrt(HDIM)
    local_len = (3 + per_block) * BLK
    global_len = seq_count * GLEN
    paired = jnp.stack([keys, values], 1)
    padded = extended(paired, (("seq", 0),), BLK)
    earlier = padded[:rows_dev].reshape(blocks_dev, BLK, 2, width_dev)
    current = paired.reshape(blocks_dev, BLK, 2, width_dev)
    later = padded[2 * BLK :].reshape(blocks_dev, BLK, 2, width_dev)
    own_global = glob_blocks[0] - my_index * blocks_dev
    mine = lax.dynamic_slice_in_dim(paired, own_global * BLK, GLEN, 0)
    global_kv = lax.all_gather(mine, "seq", axis=0, tiled=True)
    plan = rand_blocks.reshape(seq_count, spots)
    owners = plan // blocks_dev
    targets = plan % blocks_dev
    member = (owners[:, :, None] == jnp.arange(seq_count, dtype=jnp.int32)[None, None, :]).astype(
        jnp.int32
    )
    ranks = jnp.sum(member * (jnp.cumsum(member, axis=1) - 1), axis=2)
    places = owners * capacity + ranks
    my_places = lax.dynamic_index_in_dim(places, my_index, 0, keepdims=False)
    asked = (
        (owners == my_index)[:, :, None]
        & (ranks[:, :, None] == jnp.arange(capacity, dtype=jnp.int32)[None, None, :])
    ).astype(jnp.int32)
    incoming = jnp.sum(asked * (targets[:, :, None] + 1), axis=1) - 1
    block_kv = paired.reshape(blocks_dev, BLK, 2, width_dev)
    outgoing = jnp.take(block_kv, jnp.maximum(incoming, 0), axis=0)
    received = lax.all_to_all(outgoing, "seq", split_axis=0, concat_axis=0, tiled=True)
    fetched = jnp.take(received.reshape(seq_count * capacity, BLK, 2, width_dev), my_places, axis=0)
    fetched = fetched.reshape(blocks_dev, per_block * BLK, 2, width_dev)
    local_kv = jnp.concatenate([earlier, current, later, fetched], 1)
    query_blocks = queries.reshape(blocks_dev, BLK, head_count, HDIM)
    grad_blocks = out_grad.reshape(blocks_dev, BLK, head_count, HDIM)
    local_keys = local_kv[:, :, 0].reshape(blocks_dev, local_len, head_count, HDIM)
    local_vals = local_kv[:, :, 1].reshape(blocks_dev, local_len, head_count, HDIM)
    global_keys = global_kv[:, 0].reshape(global_len, head_count, HDIM)
    global_vals = global_kv[:, 1].reshape(global_len, head_count, HDIM)
    block_ids = my_index * blocks_dev + jnp.arange(blocks_dev, dtype=jnp.int32)
    before_ok = jnp.broadcast_to((block_ids > 0)[:, None], (blocks_dev, BLK))
    after_ok = jnp.broadcast_to((block_ids < total_blocks - 1)[:, None], (blocks_dev, BLK))
    visible = jnp.concatenate(
        [
            before_ok,
            jnp.ones((blocks_dev, BLK), bool),
            after_ok,
            jnp.ones((blocks_dev, per_block * BLK), bool),
        ],
        1,
    )
    scores_local = (
        jnp.einsum("bqhd,bkhd->bhqk", query_blocks, local_keys, preferred_element_type=jnp.float32)
        * scale
    )
    scores_local = jnp.where(visible[:, None, None, :], scores_local, -jnp.inf)
    scores_global = (
        jnp.einsum("bqhd,khd->bhqk", query_blocks, global_keys, preferred_element_type=jnp.float32)
        * scale
    )
    top = jnp.maximum(
        jnp.max(scores_local, axis=-1, keepdims=True),
        jnp.max(scores_global, axis=-1, keepdims=True),
    )
    expo_local = jnp.exp(scores_local - top)
    expo_global = jnp.exp(scores_global - top)
    totals = jnp.sum(expo_local, axis=-1, keepdims=True) + jnp.sum(
        expo_global, axis=-1, keepdims=True
    )
    probs_local = expo_local / totals
    probs_global = expo_global / totals
    weights_local = probs_local.astype(jnp.bfloat16)
    weights_global = probs_global.astype(jnp.bfloat16)
    attended = jnp.einsum(
        "bhqk,bkhd->bqhd", weights_local, local_vals, preferred_element_type=jnp.float32
    ) + jnp.einsum(
        "bhqk,khd->bqhd", weights_global, global_vals, preferred_element_type=jnp.float32
    )
    attn_out = attended.reshape(rows_dev, width_dev).astype(jnp.bfloat16)
    dprobs_local = jnp.einsum(
        "bqhd,bkhd->bhqk", grad_blocks, local_vals, preferred_element_type=jnp.float32
    )
    dprobs_global = jnp.einsum(
        "bqhd,khd->bhqk", grad_blocks, global_vals, preferred_element_type=jnp.float32
    )
    delta = jnp.sum(probs_local * dprobs_local, axis=-1, keepdims=True) + jnp.sum(
        probs_global * dprobs_global, axis=-1, keepdims=True
    )
    dscores_local = (probs_local * (dprobs_local - delta) * scale).astype(jnp.bfloat16)
    dscores_global = (probs_global * (dprobs_global - delta) * scale).astype(jnp.bfloat16)
    query_sum = jnp.einsum(
        "bhqk,bkhd->bqhd", dscores_local, local_keys, preferred_element_type=jnp.float32
    ) + jnp.einsum(
        "bhqk,khd->bqhd", dscores_global, global_keys, preferred_element_type=jnp.float32
    )
    query_grad = query_sum.reshape(rows_dev, width_dev).astype(jnp.bfloat16)
    local_dk = jnp.einsum(
        "bhqk,bqhd->bkhd", dscores_local, query_blocks, preferred_element_type=jnp.float32
    )
    local_dv = jnp.einsum(
        "bhqk,bqhd->bkhd", weights_local, grad_blocks, preferred_element_type=jnp.float32
    )
    local_grads = jnp.stack(
        [
            local_dk.reshape(blocks_dev, local_len, width_dev),
            local_dv.reshape(blocks_dev, local_len, width_dev),
        ],
        2,
    )
    before_terms = local_grads[:, :BLK].reshape(rows_dev, 2, width_dev)
    here_terms = local_grads[:, BLK : 2 * BLK].reshape(rows_dev, 2, width_dev)
    after_terms = local_grads[:, 2 * BLK : 3 * BLK].reshape(rows_dev, 2, width_dev)
    rims = jnp.concatenate([before_terms[:BLK], after_terms[rows_dev - BLK :]], 0)
    rim_padded = extended(rims.astype(jnp.bfloat16), (("seq", 0),), BLK).astype(rims.dtype)
    window_sum = (
        here_terms
        + jnp.concatenate([before_terms[BLK:], rim_padded[3 * BLK :]], 0)
        + jnp.concatenate([rim_padded[:BLK], after_terms[: rows_dev - BLK]], 0)
    )
    slot_grads = local_grads[:, 3 * BLK :].reshape(spots, BLK * 2 * width_dev).astype(jnp.bfloat16)
    placing = (
        my_places[:, None] == jnp.arange(seq_count * capacity, dtype=jnp.int32)[None, :]
    ).astype(jnp.bfloat16)
    to_send = jnp.einsum(
        "ts,tx->sx", placing, slot_grads, preferred_element_type=jnp.float32
    ).astype(jnp.bfloat16)
    returned = lax.all_to_all(
        to_send.reshape(seq_count, capacity, BLK * 2 * width_dev),
        "seq",
        split_axis=0,
        concat_axis=0,
        tiled=True,
    )
    landing = (
        incoming.reshape(-1)[:, None] == jnp.arange(blocks_dev, dtype=jnp.int32)[None, :]
    ).astype(jnp.bfloat16)
    random_sum = jnp.einsum(
        "sn,sx->nx",
        landing,
        returned.reshape(seq_count * capacity, BLK * 2 * width_dev),
        preferred_element_type=jnp.float32,
    ).reshape(rows_dev, 2, width_dev)
    global_dk = jnp.einsum(
        "bhqk,bqhd->khd", dscores_global, query_blocks, preferred_element_type=jnp.float32
    )
    global_dv = jnp.einsum(
        "bhqk,bqhd->khd", weights_global, grad_blocks, preferred_element_type=jnp.float32
    )
    global_terms = jnp.stack(
        [global_dk.reshape(global_len, width_dev), global_dv.reshape(global_len, width_dev)], 1
    )
    summed_all = lax.psum(global_terms, "seq")
    own_term = lax.dynamic_slice_in_dim(summed_all, my_index * GLEN, GLEN, 0)
    combined = window_sum + random_sum
    base_rows = lax.dynamic_slice_in_dim(combined, own_global * BLK, GLEN, 0)
    combined = lax.dynamic_update_slice_in_dim(combined, base_rows + own_term, own_global * BLK, 0)
    key_grad = combined[:, 0].astype(jnp.bfloat16)
    value_grad = combined[:, 1].astype(jnp.bfloat16)
    return (attn_out, query_grad, key_grad, value_grad)


def solution(mesh):
    in_specs = (
        P("seq", "head"),
        P("seq", "head"),
        P("seq", "head"),
        P("seq", "head"),
        P(),
        P("seq"),
    )
    out_specs = (P("seq", "head"), P("seq", "head"), P("seq", "head"), P("seq", "head"))
    return jax.shard_map(shards, mesh=mesh, in_specs=in_specs, out_specs=out_specs, check_vma=False)
```

profile of v0, /device:TPU:0, one launch (start us, length us, event | category | flops | bytes accessed | tf_op | source)
XLA Modules:
  0.0 270.9 jit_solution(358742052973094636)
XLA Ops:
  7.2 0.8 copy.233
  8.0 1.3 reduce_window_sum.11
  10.4 1.1 pad_maximum_fusion.6
  12.1 1.6 broadcast_select_fusion
  13.8 7.4 %all-to-all-start = ((bf16[8,2,64,2,512]{4,2,3,1,0:T(8,128)(2,1)}), bf16[8,2,64,2,512]{4,2,3,1,0:T(8,128)(2,1)S(1)}, u32[]{:S(2)}, u32[]{:S(2)}) async-start(bf16[8,2,64,2,512]{4,2,3,1,0:T(8,128)(2,1)} %broadcast_select_fusion), calls=%async_computation | async-start | bytes 4194304 | tf_op jit(solution)/shard_map/all_to_all | solution.py:62
  21.9 4.6 %collective-permute-start = (bf16[64,2,512]{2,0,1:T(8,128)(2,1)}, bf16[64,2,512]{2,0,1:T(8,128)(2,1)}, u32[]{:S(2)}, u32[]{:S(2)}) collective-permute-start(bf16[64,2,512]{2,0,1:T(8,128)(2,1)} %get-tuple-element.20), channel_id=1, source_target_pairs={{0,4},{4,8},{8,12},{12,16},{16,20},{20,24},{24,28},{1,5},{5,9},{9,... | collective-permute-start | bytes 393224 | tf_op jit(solution)/shard_map/ppermute | solution.py:19
  26.5 1.3 collective-permute-start.1
  30.2 0.8 copy.257
  31.7 61.0 %all_gather.3 = bf16[128,2,512]{2,1,0:T(2,128)(2,1)S(1)} all-gather(bf16[16,2,512]{2,1,0:T(2,128)(2,1)S(1)} %copy.241), channel_id=1, replica_groups=mesh['seq'=8,'head'=4] {'seq'}, dimensions={0}, use_global_device_ids=true | all-gather | bytes 294912 | tf_op jit(solution)/shard_map/all_gather | solution.py:45
  92.8 1.2 fusion.57
  93.9 1.1 copy.290
  95.0 1.1 copy.291
  96.4 2.0 fusion.59
  98.3 1.2 fusion.58
  99.5 0.8 copy-done.3
  100.6 1.9 pad_maximum_fusion.4
  102.4 1.9 gather_fusion.1
  104.3 1.5 copy.236
  106.1 0.8 copy-done.18
  107.2 1.4 fusion.56
  108.5 0.9 copy.238
  111.8 2.4 fusion.20
  114.3 2.7 copy.237
  116.9 1.2 fusion.54
  118.1 3.7 %fusion.1 = (f32[4,4,64]{2,1,0:T(4,128)}, f32[4,4,384,64]{2,3,1,0:T(8,128)}) fusion(f32[4,4,64]{2,1,0:T(4,128)S(1)} %copy_add_fusion.1, f32[4,4,64]{2,1,0:T(4,128)S(1)} %copy_maximum_fusion, f32[4,4,384,64]{2,3,1,0:T(8,128)S(1)} %get-tuple-element.29, bf16[4,384,4,128]{1,3,2,0:T(8,128)(2,1)} %bitcast.176, bf16[4,64,4,128]{3,2,1,0:T(4,128)(2,1)S(1)} %copy-done.17), kind=kOutput, calls=%fused_computation.15 | convolution fusion | flops 102235136 | bytes 4993024 | tf_op jit(solution)/shard_map/bqhd,bkhd->bhqk/dot_general | solution.py:112
  121.9 2.4 copy.267
  124.3 1.4 multiply_reduce_fusion
  126.4 2.4 fusion.4
  128.8 2.3 fusion.28
  131.1 3.5 %copy.266 = f32[4,384,1,512]{3,1,2,0:T(8,128)} copy(f32[4,384,1,512]{1,3,0,2:T(8,128)} %bitcast.154) | data formatting | bytes 6291456 | tf_op jit(solution)/shard_map/stack;reshape | solution.py:135
  134.7 2.3 fusion
  137.1 1.5 copy-done.6
  138.6 2.8 %copy.272 = bf16[4,192,2,512]{3,2,1,0:T(2,128)(2,1)} copy(bf16[4,192,2,512]{3,1,2,0:T(8,128)(2,1)S(1)} %slice.123) | data formatting | bytes 3145728 | tf_op jit(solution)/shard_map/slice | solution.py:152
  141.5 5.7 %convert_element_type.59 = bf16[12,65536]{1,0:T(8,128)(2,1)} reshape(bf16[4,192,2,512]{3,2,1,0:T(2,128)(2,1)} %copy.272) | data formatting | bytes 3145728 | tf_op jit(solution)/shard_map/convert_element_type | solution.py:152
  147.2 3.8 %convolution_convert_fusion = bf16[16,65536]{1,0:T(8,128)(2,1)} fusion(bf16[12,65536]{1,0:T(8,128)(2,1)} %convert_element_type.59, s32[12]{0:T(128)} %get-tuple-element.24), kind=kOutput, calls=%fused_computation.2 | convolution fusion | flops 26214592 | bytes 3670064 | tf_op jit(solution)/shard_map/ts,tx->sx/dot_general | solution.py:156
  151.0 3.6 %reshape.224 = bf16[8,2,65536]{2,1,0:T(2,128)(2,1)} reshape(bf16[16,65536]{1,0:T(8,128)(2,1)} %convolution_convert_fusion) | data formatting | bytes 4194304 | tf_op jit(solution)/shard_map/reshape | solution.py:160
  154.6 4.4 %all-to-all-start.1 = ((bf16[8,2,65536]{2,1,0:T(2,128)(2,1)}), bf16[8,2,65536]{2,1,0:T(2,128)(2,1)}, u32[]{:S(2)}, u32[]{:S(2)}) async-start(bf16[8,2,65536]{2,1,0:T(2,128)(2,1)} %reshape.224), calls=%async_computation.1 | async-start | bytes 4194304 | tf_op jit(solution)/shard_map/all_to_all | solution.py:159
  159.0 1.3 copy.271
  160.3 1.3 sub.62
  161.6 1.3 copy.260
  162.9 2.0 fusion.48
  164.9 1.8 copy.277
  166.7 1.2 convolution_bitcast_fusion.2
  168.0 2.9 %fusion.11 = bf16[4,64,4,128]{3,1,2,0:T(8,128)(2,1)S(1)} fusion(f32[4,64,4,128]{3,1,2,0:T(8,128)S(1)} %convolution_bitcast_fusion.2, bf16[4,384,4,128]{1,3,2,0:T(8,128)(2,1)} %bitcast.177, f32[4,4,384,64]{2,3,1,0:T(8,128)} %copy-done.2, f32[4,4,64]{2,1,0:T(4,128)S(1)} %copy_add_fusion.1, f32[4,4,64]{2,1,0:T(4,128)S(1)} %copy_maximum_fusion), kind=kOutput, calls=%fused_computation.33 | convolution fusion | flops 102105088 | bytes 3940352 | tf_op jit(solution)/shard_map/bhqk,bkhd->bqhd/dot_general | solution.py:106
  172.1 1.0 fusion.50
  173.0 1.9 copy.276
  174.9 1.9 pad_maximum_fusion.7
  177.0 2.6 fusion.10
  180.7 1.1 copy.268
  181.7 1.0 slice_bitcast_fusion.3
  182.7 3.8 %collective-permute-start.2 = (bf16[64,2,512]{2,0,1:T(8,128)(2,1)S(1)}, bf16[64,2,512]{2,0,1:T(8,128)(2,1)S(1)}, u32[]{:S(2)}, u32[]{:S(2)}) collective-permute-start(bf16[64,2,512]{2,0,1:T(8,128)(2,1)S(1)} %get-tuple-element.10), channel_id=1, source_target_pairs={{0,4},{4,8},{8,12},{12,16},{16,20},{20,24},{24,28},{1,5},{5,9},{9,... | collective-permute-start | bytes 393224 | tf_op jit(solution)/shard_map/ppermute | solution.py:19
  186.5 1.3 collective-permute-start.3
  188.0 0.9 copy.270
  188.9 0.9 copy.269
  189.8 4.0 %collective-permute-done.3 = bf16[64,2,512]{2,0,1:T(8,128)(2,1)S(1)} collective-permute-done((bf16[64,2,512]{2,0,1:T(8,128)(2,1)S(1)}, bf16[64,2,512]{2,0,1:T(8,128)(2,1)S(1)}, u32[]{:S(2)}, u32[]{:S(2)}) %collective-permute-start.3) | collective-permute-done | bytes 131104 | tf_op jit(solution)/shard_map/ppermute | solution.py:20
  193.8 0.8 fusion.33
  194.6 15.2 %all-to-all-done.1 = bf16[8,2,65536]{2,1,0:T(2,128)(2,1)} async-done(((bf16[8,2,65536]{2,1,0:T(2,128)(2,1)}), bf16[8,2,65536]{2,1,0:T(2,128)(2,1)}, u32[]{:S(2)}, u32[]{:S(2)}) %all-to-all-start.1) | async-done | bytes 2097184 | tf_op jit(solution)/shard_map/all_to_all | solution.py:159
  209.8 2.1 reshape.225
  211.8 1.6 fusion.37
  213.4 2.4 reshape.226
  215.8 1.9 fusion.14
  217.7 44.7 %all-reduce.2.cloned.1.call-done = f32[128,2,512]{2,0,1:T(8,128)} async-done(((f32[128,2,512]{2,0,1:T(8,128)}), f32[128,2,512]{2,0,1:T(8,128)}) %all-reduce.2.cloned.1.call-update) | async-done | bytes 524304 | tf_op jit(solution)/shard_map/psum | solution.py:184
  262.4 0.9 add_dynamic-update-slice_fusion
  263.3 0.8 slice_bitcast_fusion
  (111 shorter events, 11.9 us)
Async XLA Ops:
  13.8 7.4 %copy-start.8 = (bf16[256,512]{1,0:T(8,128)(2,1)S(1)}, bf16[256,512]{1,0:T(8,128)(2,1)}, u32[]{:S(2)}) copy-start(bf16[256,512]{1,0:T(8,128)(2,1)} %param.7) | copy-start | bytes 786436
  13.8 7.4 %copy-start.9 = (bf16[256,512]{1,0:T(8,128)(2,1)S(1)}, bf16[256,512]{1,0:T(8,128)(2,1)}, u32[]{:S(2)}) copy-start(bf16[256,512]{1,0:T(8,128)(2,1)} %param.8) | copy-start | bytes 786436
  13.8 88.7 %all-to-all-start = ((bf16[8,2,64,2,512]{4,2,3,1,0:T(8,128)(2,1)}), bf16[8,2,64,2,512]{4,2,3,1,0:T(8,128)(2,1)S(1)}, u32[]{:S(2)}, u32[]{:S(2)}) async-start(bf16[8,2,64,2,512]{4,2,3,1,0:T(8,128)(2,1)} %broadcast_select_fusion), calls=%async_computation | async-start | bytes 4194304 | tf_op jit(solution)/shard_map/all_to_all | solution.py:62
  21.1 8.9 %copy-start.20 = (bf16[256,512]{1,0:T(8,128)(2,1)S(1)}, bf16[256,512]{1,0:T(8,128)(2,1)}, u32[]{:S(2)}) copy-start(bf16[256,512]{1,0:T(8,128)(2,1)} %param.6) | copy-start | bytes 786436
  21.1 9.0 %copy-start.21 = (bf16[256,512]{1,0:T(8,128)(2,1)S(1)}, bf16[256,512]{1,0:T(8,128)(2,1)}, u32[]{:S(2)}) copy-start(bf16[256,512]{1,0:T(8,128)(2,1)} %param.9) | copy-start | bytes 786436
  21.9 78.6 %collective-permute-start = (bf16[64,2,512]{2,0,1:T(8,128)(2,1)}, bf16[64,2,512]{2,0,1:T(8,128)(2,1)}, u32[]{:S(2)}, u32[]{:S(2)}) collective-permute-start(bf16[64,2,512]{2,0,1:T(8,128)(2,1)} %get-tuple-element.20), channel_id=1, source_target_pairs={{0,4},{4,8},{8,12},{12,16},{16,20},{20,24},{24,28},{1,5},{5,9},{9,... | collective-permute-start | bytes 393224 | tf_op jit(solution)/shard_map/ppermute | solution.py:19
  26.5 74.1 %collective-permute-start.1 = (bf16[64,2,512]{2,0,1:T(8,128)(2,1)}, bf16[64,2,512]{2,0,1:T(8,128)(2,1)}, u32[]{:S(2)}, u32[]{:S(2)}) collective-permute-start(bf16[64,2,512]{2,0,1:T(8,128)(2,1)} %get-tuple-element.21), channel_id=1, source_target_pairs={{4,0},{8,4},{12,8},{16,12},{20,16},{24,20},{28,24},{5,1},{9,5},{13... | collective-permute-start | bytes 393224 | tf_op jit(solution)/shard_map/ppermute | solution.py:20
  30.2 65.9 %copy-start.15 = (bf16[4,64,4,128]{3,2,1,0:T(4,128)(2,1)}, bf16[4,64,4,128]{3,2,1,0:T(4,128)(2,1)S(1)}, u32[]{:S(2)}) copy-start(bf16[4,64,4,128]{3,2,1,0:T(4,128)(2,1)S(1)} %reshape.222) | copy-start | bytes 786436
  96.1 4.4 %copy-start.19 = (bf16[128,1,512]{0,2,1:T(8,128)(2,1)}, bf16[128,1,512]{0,2,1:T(8,128)(2,1)S(1)}, u32[]{:S(2)}) copy-start(bf16[128,1,512]{0,2,1:T(8,128)(2,1)S(1)} %copy.291) | copy-start | bytes 393220
  99.5 0.8 copy-start.3
  104.3 1.5 copy-start.24
  105.9 1.0 copy-start.18
  109.4 1.1 copy-start.1
  109.4 1.4 copy-start.4
  110.5 7.6 %copy-start.2 = (f32[4,4,384,64]{2,3,1,0:T(8,128)}, f32[4,4,384,64]{2,3,1,0:T(8,128)S(1)}, u32[]{:S(2)}) copy-start(f32[4,4,384,64]{2,3,1,0:T(8,128)S(1)} %get-tuple-element.29) | copy-start | bytes 4718596
  110.6 1.3 copy-start.16
  114.3 2.7 copy-start.5
  114.3 3.9 %copy-start.17 = (bf16[4,64,4,128]{3,2,1,0:T(4,128)(2,1)S(1)}, bf16[4,64,4,128]{3,2,1,0:T(4,128)(2,1)}, u32[]{:S(2)}) copy-start(bf16[4,64,4,128]{3,2,1,0:T(4,128)(2,1)} %copy-done.15) | copy-start | bytes 786436
  126.4 2.4 copy-start.22
  128.8 2.3 copy-start.7
  136.9 1.7 copy-start.6
  154.6 55.2 %all-to-all-start.1 = ((bf16[8,2,65536]{2,1,0:T(2,128)(2,1)}), bf16[8,2,65536]{2,1,0:T(2,128)(2,1)}, u32[]{:S(2)}, u32[]{:S(2)}) async-start(bf16[8,2,65536]{2,1,0:T(2,128)(2,1)} %reshape.224), calls=%async_computation.1 | async-start | bytes 4194304 | tf_op jit(solution)/shard_map/all_to_all | solution.py:159
  159.0 103.4 %all-reduce.2.cloned.1.call-start = ((), (), s32[]{:S(2)}) async-start(), calls=%async_computation.2 | async-start | bytes 1048576 | tf_op jit(solution)/shard_map/psum | solution.py:184
  168.0 3.9 %copy-start.10 = (f32[4,128,256]{1,2,0:S(1)}, f32[4,128,256]{1,2,0}, u32[]{:S(2)}) copy-start(f32[4,128,256]{1,2,0} %fusion.59) | copy-start | bytes 1572868
  168.0 3.9 %copy-start.11 = (f32[4,4,64,128]{3,2,0,1:T(8,128)S(1)}, f32[4,4,64,128]{3,2,0,1:T(8,128)}, u32[]{:S(2)}) copy-start(f32[4,4,64,128]{3,2,0,1:T(8,128)} %get-tuple-element.5) | copy-start | bytes 1572868
  168.0 3.9 %copy-start.23 = (f32[4,4,64]{2,0,1:T(4,128)S(1)}, f32[4,4,64]{2,0,1:T(4,128)}, u32[]{:S(2)}) copy-start(f32[4,4,64]{2,0,1:T(4,128)} %copy.260) | copy-start | bytes 12292
  172.0 1.0 copy-start.13
  173.0 3.7 %copy-start.14 = (bf16[4,4,64,128]{3,2,0,1:T(8,128)(2,1)S(1)}, bf16[4,4,64,128]{3,2,0,1:T(8,128)(2,1)}, u32[]{:S(2)}) copy-start(bf16[4,4,64,128]{3,2,0,1:T(8,128)(2,1)} %copy-done.13) | copy-start | bytes 786436
  177.0 3.5 %copy-start = (f32[4,384,1,512]{3,1,2,0:T(8,128)S(1)}, f32[4,384,1,512]{3,1,2,0:T(8,128)}, u32[]{:S(2)}) copy-start(f32[4,384,1,512]{3,1,2,0:T(8,128)} %copy.266) | copy-start | bytes 9437188
  182.7 7.1 %collective-permute-start.2 = (bf16[64,2,512]{2,0,1:T(8,128)(2,1)S(1)}, bf16[64,2,512]{2,0,1:T(8,128)(2,1)S(1)}, u32[]{:S(2)}, u32[]{:S(2)}) collective-permute-start(bf16[64,2,512]{2,0,1:T(8,128)(2,1)S(1)} %get-tuple-element.10), channel_id=1, source_target_pairs={{0,4},{4,8},{8,12},{12,16},{16,20},{20,24},{24,28},{1,5},{5,9},{9,... | collective-permute-start | bytes 393224 | tf_op jit(solution)/shard_map/ppermute | solution.py:19
  186.5 7.3 %collective-permute-start.3 = (bf16[64,2,512]{2,0,1:T(8,128)(2,1)S(1)}, bf16[64,2,512]{2,0,1:T(8,128)(2,1)S(1)}, u32[]{:S(2)}, u32[]{:S(2)}) collective-permute-start(bf16[64,2,512]{2,0,1:T(8,128)(2,1)S(1)} %get-tuple-element.11), channel_id=1, source_target_pairs={{4,0},{8,4},{12,8},{16,12},{20,16},{24,20},{28,24},{5,1},{9,5},{13... | collective-permute-start | bytes 393224 | tf_op jit(solution)/shard_map/ppermute | solution.py:20
  194.6 17.3 %copy-start.25 = (s32[16]{0:T(128)S(1)}, s32[16]{0:T(128)}, u32[]{:S(2)}) copy-start(s32[16]{0:T(128)} %sub.62) | copy-start | bytes 196
  213.4 2.4 copy-start.12
Sparse Core Ops, SparseCore 0:
  176.9 85.3 all-reduce.1
where the time goes:
time: 272 us; the launch traced here: 271 us
  waiting for transfers between devices  63.9 us (23%)
  blocking collectives  61 us (22%)
  local copies, waits for them, and re-layouts  57.8 us (21%)
  matrix products  27.4 us (10%)
  other arithmetic  23 us (8%)
  starting transfers between devices  22.7 us (8%)
  between operations  15.2 us (6%)
    all_gather x1, blocking collectives, shards(): global_kv = lax.all_gather(mine, 'seq', axis=0, tiled=True)  61 us
    psum x1, waiting for transfers between devices, shards(): summed_all = lax.psum(global_terms, 'seq')  44.7 us
    all_to_all x1, waiting for transfers between devices, shards(): lax.all_to_all(to_send.reshape(seq_count, capacity, BLK * 2 * width_dev),...  15.2 us
    unnamed x57, local copies, waits for them, and re-layouts  8.55 us
    ppermute x2, starting transfers between devices, extended(): before = lax.ppermute(last, axis, up)  8.31 us
    all_to_all x1, starting transfers between devices, shards(): lax.all_to_all(outgoing, 'seq', split_axis=0, concat_axis=0, tiled=True)  7.38 us
    another operation x2, local copies, waits for them, and re-layouts, shards(): jnp.stack([local_dk.reshape(blocks_dev, local_len, width_dev), local_dv.r...  5.89 us
    convert_element_type x1, local copies, waits for them, and re-layouts, shards(): local_grads[:, 3 * BLK:].reshape(spots, BLK * 2 * width_dev)  5.73 us
  transfers between devices with their start and end apart: 7, of which 3 were waited for; matrix products, arithmetic and copies ran while one was open for 17% of the time, Pallas kernels for 0%

commit v1 on v0

--- a/solution.py
+++ b/solution.py
@@ -42,7 +42,16 @@
     later = padded[2 * BLK :].reshape(blocks_dev, BLK, 2, width_dev)
     own_global = glob_blocks[0] - my_index * blocks_dev
     mine = lax.dynamic_slice_in_dim(paired, own_global * BLK, GLEN, 0)
-    global_kv = lax.all_gather(mine, "seq", axis=0, tiled=True)
+    ways = lax.axis_size("seq")
+    up_2 = [(d, (d + 1) % ways) for d in range(ways)]
+    down_2 = [(d, (d - 1) % ways) for d in range(ways)]
+    earlier_2, later_2 = ([mine], [mine])
+    for _ in range(ways // 2):
+        earlier_2.append(lax.ppermute(earlier_2[-1], "seq", up_2))
+    for _ in range((ways - 1) // 2):
+        later_2.append(lax.ppermute(later_2[-1], "seq", down_2))
+    line = jnp.concatenate([*earlier_2[::-1], *later_2[1:]], axis=0)
+    global_kv = jnp.roll(line, (lax.axis_index("seq") - ways // 2) * mine.shape[0], axis=0)
     plan = rand_blocks.reshape(seq_count, spots)
     owners = plan // blocks_dev
     targets = plan % blocks_dev

time: 272 us -> 290 us (1.066)
  blocking collectives: 61 us -> 0 us
  waiting for transfers between devices: 63.9 us -> 108 us
  starting transfers between devices: 22.7 us -> 49.1 us
  local copies, waits for them, and re-layouts: 57.8 us -> 66.8 us
    all_gather x1 -> x0, blocking collectives: 61 us -> none  [shards(): global_kv = lax.all_gather(mine, 'seq', axis=0, tiled=True)]
    ppermute x0 -> x7, waiting for transfers between devices: none -> 44.9 us  [the longest x4 42.7 us: shards(): earlier_2.append(lax.ppermute(earlier_2[-1], 'seq', up_2))]
    ppermute x0 -> x7, starting transfers between devices: none -> 26.1 us  [the longest x3 14.9 us: shards(): later_2.append(lax.ppermute(later_2[-1], 'seq', down_2))]
    concatenate x0 -> x1, local copies, waits for them, and re-layouts: none -> 5.44 us  [shards(): jnp.roll(line, (lax.axis_index('seq') - ways // 2) * mine.shape[0], axis=0)]
    psum x1, waiting for transfers between devices: 44.7 us -> 40.2 us  [shards(): summed_all = lax.psum(global_terms, 'seq')]
    slice x1 -> x3, local copies, waits for them, and re-layouts: 1.15 us -> 4.57 us  [the longest x1 2.06 us: shards(): later = padded[2 * BLK:].reshape(blocks_dev, BLK, 2, width_dev)]
    unnamed x57 -> x71, local copies, waits for them, and re-layouts: 8.55 us -> 6.75 us
  transfers between devices with their start and end apart: 7 -> 14, of which waited for: 3 -> 9; matrix products, arithmetic and copies ran while one was open for 17% -> 19% of each run, Pallas kernels for 0% -> 0%
where the time goes in v1:
time: 290 us; the launch traced here: 289 us
  waiting for transfers between devices  108 us (37%)
  local copies, waits for them, and re-layouts  66.8 us (23%)
  starting transfers between devices  49.1 us (17%)
  matrix products  25.3 us (9%)
  other arithmetic  24.2 us (8%)
  between operations  15.3 us (5%)
    ppermute x4, waiting for transfers between devices, shards(): earlier_2.append(lax.ppermute(earlier_2[-1], 'seq', up_2))  42.7 us
    psum x1, waiting for transfers between devices, shards(): summed_all = lax.psum(global_terms, 'seq')  40.2 us
    all_to_all x1, waiting for transfers between devices, shards(): lax.all_to_all(to_send.reshape(seq_count, capacity, BLK * 2 * width_dev),...  17.7 us
    ppermute x3, starting transfers between devices, shards(): later_2.append(lax.ppermute(later_2[-1], 'seq', down_2))  14.9 us
    ppermute x4, starting transfers between devices, shards(): earlier_2.append(lax.ppermute(earlier_2[-1], 'seq', up_2))  11.2 us
    all_to_all x1, starting transfers between devices, shards(): lax.all_to_all(outgoing, 'seq', split_axis=0, concat_axis=0, tiled=True)  7.38 us
    unnamed x71, local copies, waits for them, and re-layouts  6.75 us
    ppermute x2, starting transfers between devices, extended(): before = lax.ppermute(last, axis, up)  6.72 us
  transfers between devices with their start and end apart: 14, of which 9 were waited for; matrix products, arithmetic and copies ran while one was open for 19% of the time, Pallas kernels for 0%

profile of v1, /device:TPU:0, one launch (start us, length us, event | category | flops | bytes accessed | tf_op | source)
XLA Modules:
  0.0 288.8 jit_solution(102366162480503696)
XLA Ops:
  8.0 1.3 reduce_window_sum.11
  10.4 1.1 pad_maximum_fusion.6
  12.2 1.6 broadcast_select_fusion
  13.8 7.4 %all-to-all-start = ((bf16[8,2,64,2,512]{4,2,3,1,0:T(8,128)(2,1)}), bf16[8,2,64,2,512]{4,2,3,1,0:T(8,128)(2,1)S(1)}, u32[]{:S(2)}, u32[]{:S(2)}) async-start(bf16[8,2,64,2,512]{4,2,3,1,0:T(8,128)(2,1)} %broadcast_select_fusion), calls=%async_computation | async-start | bytes 4194304 | tf_op jit(solution)/shard_map/all_to_all | solution.py:71
  22.3 4.8 %collective-permute-start.6 = (bf16[16,2,512]{0,2,1:T(8,128)(2,1)S(1)}, bf16[16,2,512]{0,2,1:T(8,128)(2,1)}, u32[]{:S(2)}, u32[]{:S(2)}) collective-permute-start(bf16[16,2,512]{0,2,1:T(8,128)(2,1)S(1)} %fusion.23), channel_id=1, source_target_pairs={{0,28},{4,0},{8,4},{12,8},{16,12},{20,16},{24,20},{28,24},{1,29},{... | collective-permute-start | bytes 98312 | tf_op jit(solution)/shard_map/ppermute | solution.py:52
  28.0 2.8 collective-permute-start
  30.8 1.3 collective-permute-start.1
  33.0 32.8 %collective-permute-done.2 = bf16[16,2,512]{0,2,1:T(8,128)(2,1)S(1)} collective-permute-done((bf16[16,2,512]{0,2,1:T(8,128)(2,1)S(1)}, bf16[16,2,512]{0,2,1:T(8,128)(2,1)S(1)}, u32[]{:S(2)}, u32[]{:S(2)}) %collective-permute-start.2) | collective-permute-done | bytes 32800 | tf_op jit(solution)/shard_map/ppermute | solution.py:50
  65.8 4.8 %collective-permute-start.7 = (bf16[16,2,512]{0,2,1:T(8,128)(2,1)}, bf16[16,2,512]{0,2,1:T(8,128)(2,1)}, u32[]{:S(2)}, u32[]{:S(2)}) collective-permute-start(bf16[16,2,512]{0,2,1:T(8,128)(2,1)} %collective-permute-done.6), channel_id=1, source_target_pairs={{0,28},{4,0},{8,4},{12,8},{16,12},{20,16},{24,20},{28,24},{1,29},{... | collective-permute-start | bytes 98312 | tf_op jit(solution)/shard_map/ppermute | solution.py:52
  70.6 5.0 %collective-permute-done.3 = bf16[16,2,512]{0,2,1:T(8,128)(2,1)} collective-permute-done((bf16[16,2,512]{0,2,1:T(8,128)(2,1)S(1)}, bf16[16,2,512]{0,2,1:T(8,128)(2,1)}, u32[]{:S(2)}, u32[]{:S(2)}) %collective-permute-start.3) | collective-permute-done | bytes 32800 | tf_op jit(solution)/shard_map/ppermute | solution.py:50
  75.6 2.9 %collective-permute-start.4 = (bf16[16,2,512]{0,2,1:T(8,128)(2,1)}, bf16[16,2,512]{0,2,1:T(8,128)(2,1)}, u32[]{:S(2)}, u32[]{:S(2)}) collective-permute-start(bf16[16,2,512]{0,2,1:T(8,128)(2,1)} %collective-permute-done.3), channel_id=1, source_target_pairs={{0,4},{4,8},{8,12},{12,16},{16,20},{20,24},{24,28},{28,0},{1,5},{5... | collective-permute-start | bytes 98312 | tf_op jit(solution)/shard_map/ppermute | solution.py:50
  79.3 1.0 reshape.221
  80.3 1.0 reshape.222
  82.9 5.4 %collective-permute-start.8 = (bf16[16,2,512]{0,2,1:T(8,128)(2,1)}, bf16[16,2,512]{0,2,1:T(8,128)(2,1)}, u32[]{:S(2)}, u32[]{:S(2)}) collective-permute-start(bf16[16,2,512]{0,2,1:T(8,128)(2,1)} %collective-permute-done.7), channel_id=1, source_target_pairs={{0,28},{4,0},{8,4},{12,8},{16,12},{20,16},{24,20},{28,24},{1,29},{... | collective-permute-start | bytes 98312 | tf_op jit(solution)/shard_map/ppermute | solution.py:52
  88.3 2.4 collective-permute-done.4
  90.7 8.3 %collective-permute-start.5 = (bf16[16,2,512]{0,2,1:T(8,128)(2,1)}, bf16[16,2,512]{0,2,1:T(8,128)(2,1)}, u32[]{:S(2)}, u32[]{:S(2)}) collective-permute-start(bf16[16,2,512]{0,2,1:T(8,128)(2,1)} %collective-permute-done.4), channel_id=1, source_target_pairs={{0,4},{4,8},{8,12},{12,16},{16,20},{20,24},{24,28},{28,0},{1,5},{5... | collective-permute-start | bytes 98312 | tf_op jit(solution)/shard_map/ppermute | solution.py:50
  99.0 2.5 pad_maximum_fusion.4
  101.5 1.3 copy.197
  102.8 2.1 copy.198
  104.9 2.2 collective-permute-done.8
  107.0 2.5 collective-permute-done.5
  109.5 5.4 %concatenate.36 = bf16[256,2,512]{0,2,1:T(8,128)(2,1)} concatenate(bf16[16,2,512]{0,2,1:T(8,128)(2,1)} %collective-permute-done.5, bf16[16,2,512]{0,2,1:T(8,128)(2,1)} %collective-permute-done.4, bf16[16,2,512]{0,2,1:T(8,128)(2,1)} %collective-permute-done.3, bf16[16,2,512]{0,2,1:T(8,128)(2,1)S(1)} %copy-done.25, bf16[16,2,512]{0,2,1:T(8,128)(2,1)S(1)} %fusion.23, ...), dimensions={0} | concatenate | bytes 1048576 | tf_op jit(solution)/shard_map/jit(_roll_dynamic)/concatenate | solution.py:54
  115.0 1.2 constant_dynamic-slice_fusion.1
  116.2 1.2 fusion.57
  118.5 1.0 fusion.58
  119.5 1.9 gather_fusion.1
  121.4 1.6 copy.202
  124.5 1.4 fusion.56
  129.1 2.4 fusion.20
  131.5 2.7 copy.203
  134.2 1.2 fusion.54
  135.4 3.7 %fusion.1 = (f32[4,4,64]{2,1,0:T(4,128)}, f32[4,4,384,64]{2,3,1,0:T(8,128)}) fusion(f32[4,4,64]{2,1,0:T(4,128)S(1)} %copy_add_fusion.1, f32[4,4,64]{2,1,0:T(4,128)S(1)} %copy_maximum_fusion, f32[4,4,384,64]{2,3,1,0:T(8,128)S(1)} %get-tuple-element.29, bf16[4,384,4,128]{1,3,2,0:T(8,128)(2,1)} %bitcast.176, bf16[4,64,4,128]{3,2,1,0:T(4,128)(2,1)S(1)} %copy-done.13), kind=kOutput, calls=%fused_computation.15 | convolution fusion | flops 102235136 | bytes 4993024 | tf_op jit(solution)/shard_map/bqhd,bkhd->bhqk/dot_general | solution.py:121
  139.2 2.4 copy.230
  141.5 1.4 multiply_reduce_fusion
  143.7 2.4 fusion.4
  146.1 2.3 fusion.31
  148.4 3.5 %copy.229 = f32[4,384,1,512]{3,1,2,0:T(8,128)} copy(f32[4,384,1,512]{1,3,0,2:T(8,128)} %bitcast.154) | data formatting | bytes 6291456 | tf_op jit(solution)/shard_map/stack;reshape | solution.py:144
  151.9 2.3 fusion
  154.4 1.5 copy-done.6
  155.9 2.8 copy.235
  158.7 5.8 %convert_element_type.59 = bf16[12,65536]{1,0:T(8,128)(2,1)} reshape(bf16[4,192,2,512]{3,2,1,0:T(2,128)(2,1)} %copy.235) | data formatting | bytes 3145728 | tf_op jit(solution)/shard_map/convert_element_type | solution.py:161
  164.5 3.8 %convolution_convert_fusion = bf16[16,65536]{1,0:T(8,128)(2,1)} fusion(bf16[12,65536]{1,0:T(8,128)(2,1)} %convert_element_type.59, s32[12]{0:T(128)} %get-tuple-element.24), kind=kOutput, calls=%fused_computation.2 | convolution fusion | flops 26214592 | bytes 3670064 | tf_op jit(solution)/shard_map/ts,tx->sx/dot_general | solution.py:165
  168.2 3.6 %reshape.224 = bf16[8,2,65536]{2,1,0:T(2,128)(2,1)} reshape(bf16[16,65536]{1,0:T(8,128)(2,1)} %convolution_convert_fusion) | data formatting | bytes 4194304 | tf_op jit(solution)/shard_map/reshape | solution.py:169
  171.9 6.2 %all-to-all-start.1 = ((bf16[8,2,65536]{2,1,0:T(2,128)(2,1)}), bf16[8,2,65536]{2,1,0:T(2,128)(2,1)}, u32[]{:S(2)}, u32[]{:S(2)}) async-start(bf16[8,2,65536]{2,1,0:T(2,128)(2,1)} %reshape.224), calls=%async_computation.1 | async-start | bytes 4194304 | tf_op jit(solution)/shard_map/all_to_all | solution.py:168
  178.1 1.3 copy.234
  179.5 1.3 sub.71
  180.8 1.3 copy.223
  182.1 2.0 fusion.48
  184.1 1.8 copy.240
  185.9 2.8 convolution_bitcast_fusion.3
  191.2 1.8 copy.239
  193.0 2.5 convolution_bitcast_fusion.1
  197.6 1.3 fusion.12
  198.9 1.0 copy.231
  200.9 3.9 %collective-permute-start.9 = (bf16[64,2,512]{2,0,1:T(8,128)(2,1)S(1)}, bf16[64,2,512]{2,0,1:T(8,128)(2,1)S(1)}, u32[]{:S(2)}, u32[]{:S(2)}) collective-permute-start(bf16[64,2,512]{2,0,1:T(8,128)(2,1)S(1)} %get-tuple-element.10), channel_id=1, source_target_pairs={{0,4},{4,8},{8,12},{12,16},{16,20},{20,24},{24,28},{1,5},{5,9},{9,... | collective-permute-start | bytes 393224 | tf_op jit(solution)/shard_map/ppermute | solution.py:19
  204.8 1.3 collective-permute-start.10
  208.2 1.6 collective-permute-done.9
  209.7 3.9 %collective-permute-done.10 = bf16[64,2,512]{2,0,1:T(8,128)(2,1)S(1)} collective-permute-done((bf16[64,2,512]{2,0,1:T(8,128)(2,1)S(1)}, bf16[64,2,512]{2,0,1:T(8,128)(2,1)S(1)}, u32[]{:S(2)}, u32[]{:S(2)}) %collective-permute-start.10) | collective-permute-done | bytes 131104 | tf_op jit(solution)/shard_map/ppermute | solution.py:20
  214.4 17.7 %all-to-all-done.1 = bf16[8,2,65536]{2,1,0:T(2,128)(2,1)} async-done(((bf16[8,2,65536]{2,1,0:T(2,128)(2,1)}), bf16[8,2,65536]{2,1,0:T(2,128)(2,1)}, u32[]{:S(2)}, u32[]{:S(2)}) %all-to-all-start.1) | async-done | bytes 2097184 | tf_op jit(solution)/shard_map/all_to_all | solution.py:168
  232.1 2.1 reshape.225
  234.2 1.5 fusion.37
  235.8 2.4 reshape.226
  238.2 1.9 fusion.14
  240.1 40.2 %all-reduce.2.cloned.1.call-done = f32[128,2,512]{2,0,1:T(8,128)} async-done(((f32[128,2,512]{2,0,1:T(8,128)}), f32[128,2,512]{2,0,1:T(8,128)}) %all-reduce.2.cloned.1.call-update) | async-done | bytes 524304 | tf_op jit(solution)/shard_map/psum | solution.py:193
  (140 shorter events, 23.8 us)
Async XLA Ops:
  13.8 7.4 %copy-start.18 = (bf16[256,512]{1,0:T(8,128)(2,1)S(1)}, bf16[256,512]{1,0:T(8,128)(2,1)}, u32[]{:S(2)}) copy-start(bf16[256,512]{1,0:T(8,128)(2,1)} %param.7) | copy-start | bytes 786436
  13.8 7.5 %copy-start.16 = (bf16[256,512]{1,0:T(8,128)(2,1)S(1)}, bf16[256,512]{1,0:T(8,128)(2,1)}, u32[]{:S(2)}) copy-start(bf16[256,512]{1,0:T(8,128)(2,1)} %param.8) | copy-start | bytes 786436
  13.8 105.7 %all-to-all-start = ((bf16[8,2,64,2,512]{4,2,3,1,0:T(8,128)(2,1)}), bf16[8,2,64,2,512]{4,2,3,1,0:T(8,128)(2,1)S(1)}, u32[]{:S(2)}, u32[]{:S(2)}) async-start(bf16[8,2,64,2,512]{4,2,3,1,0:T(8,128)(2,1)} %broadcast_select_fusion), calls=%async_computation | async-start | bytes 4194304 | tf_op jit(solution)/shard_map/all_to_all | solution.py:71
  22.3 43.5 %collective-permute-start.6 = (bf16[16,2,512]{0,2,1:T(8,128)(2,1)S(1)}, bf16[16,2,512]{0,2,1:T(8,128)(2,1)}, u32[]{:S(2)}, u32[]{:S(2)}) collective-permute-start(bf16[16,2,512]{0,2,1:T(8,128)(2,1)S(1)} %fusion.23), channel_id=1, source_target_pairs={{0,28},{4,0},{8,4},{12,8},{16,12},{20,16},{24,20},{28,24},{1,29},{... | collective-permute-start | bytes 98312 | tf_op jit(solution)/shard_map/ppermute | solution.py:52
  27.1 38.7 %collective-permute-start.2 = (bf16[16,2,512]{0,2,1:T(8,128)(2,1)S(1)}, bf16[16,2,512]{0,2,1:T(8,128)(2,1)S(1)}, u32[]{:S(2)}, u32[]{:S(2)}) collective-permute-start(bf16[16,2,512]{0,2,1:T(8,128)(2,1)S(1)} %fusion.23), channel_id=1, source_target_pairs={{0,4},{4,8},{8,12},{12,16},{16,20},{20,24},{24,28},{28,0},{1,5},{5... | collective-permute-start | bytes 98312 | tf_op jit(solution)/shard_map/ppermute | solution.py:50
  28.0 71.0 %collective-permute-start = (bf16[64,2,512]{0,2,1:T(8,128)(2,1)}, bf16[64,2,512]{0,2,1:T(8,128)(2,1)}, u32[]{:S(2)}, u32[]{:S(2)}) collective-permute-start(bf16[64,2,512]{0,2,1:T(8,128)(2,1)} %get-tuple-element.22), channel_id=1, source_target_pairs={{0,4},{4,8},{8,12},{12,16},{16,20},{20,24},{24,28},{1,5},{5,9},{9,... | collective-permute-start | bytes 393224 | tf_op jit(solution)/shard_map/ppermute | solution.py:19
  30.8 68.2 %collective-permute-start.1 = (bf16[64,2,512]{0,2,1:T(8,128)(2,1)}, bf16[64,2,512]{0,2,1:T(8,128)(2,1)}, u32[]{:S(2)}, u32[]{:S(2)}) collective-permute-start(bf16[64,2,512]{0,2,1:T(8,128)(2,1)} %get-tuple-element.23), channel_id=1, source_target_pairs={{4,0},{8,4},{12,8},{16,12},{20,16},{24,20},{28,24},{5,1},{9,5},{13... | collective-permute-start | bytes 393224 | tf_op jit(solution)/shard_map/ppermute | solution.py:20
  65.8 13.5 %copy-start.24 = (bf16[16,2,512]{0,2,1:T(8,128)(2,1)}, bf16[16,2,512]{0,2,1:T(8,128)(2,1)S(1)}, u32[]{:S(2)}) copy-start(bf16[16,2,512]{0,2,1:T(8,128)(2,1)S(1)} %collective-permute-done.2) | copy-start | bytes 98308
  65.8 9.8 %collective-permute-start.3 = (bf16[16,2,512]{0,2,1:T(8,128)(2,1)S(1)}, bf16[16,2,512]{0,2,1:T(8,128)(2,1)}, u32[]{:S(2)}, u32[]{:S(2)}) collective-permute-start(bf16[16,2,512]{0,2,1:T(8,128)(2,1)S(1)} %collective-permute-done.2), channel_id=1, source_target_pairs={{0,4},{4,8},{8,12},{12,16},{16,20},{20,24},{24,28},{28,0},{1,5},{5... | collective-permute-start | bytes 98312 | tf_op jit(solution)/shard_map/ppermute | solution.py:50
  65.8 17.0 %collective-permute-start.7 = (bf16[16,2,512]{0,2,1:T(8,128)(2,1)}, bf16[16,2,512]{0,2,1:T(8,128)(2,1)}, u32[]{:S(2)}, u32[]{:S(2)}) collective-permute-start(bf16[16,2,512]{0,2,1:T(8,128)(2,1)} %collective-permute-done.6), channel_id=1, source_target_pairs={{0,28},{4,0},{8,4},{12,8},{16,12},{20,16},{24,20},{28,24},{1,29},{... | collective-permute-start | bytes 98312 | tf_op jit(solution)/shard_map/ppermute | solution.py:52
  75.6 15.1 %collective-permute-start.4 = (bf16[16,2,512]{0,2,1:T(8,128)(2,1)}, bf16[16,2,512]{0,2,1:T(8,128)(2,1)}, u32[]{:S(2)}, u32[]{:S(2)}) collective-permute-start(bf16[16,2,512]{0,2,1:T(8,128)(2,1)} %collective-permute-done.3), channel_id=1, source_target_pairs={{0,4},{4,8},{8,12},{12,16},{16,20},{20,24},{24,28},{28,0},{1,5},{5... | collective-permute-start | bytes 98312 | tf_op jit(solution)/shard_map/ppermute | solution.py:50
  81.3 20.2 %copy-start.11 = (bf16[4,64,4,128]{3,2,1,0:T(4,128)(2,1)}, bf16[4,64,4,128]{3,2,1,0:T(4,128)(2,1)S(1)}, u32[]{:S(2)}) copy-start(bf16[4,64,4,128]{3,2,1,0:T(4,128)(2,1)S(1)} %reshape.222) | copy-start | bytes 786436
  82.9 24.2 %collective-permute-start.8 = (bf16[16,2,512]{0,2,1:T(8,128)(2,1)}, bf16[16,2,512]{0,2,1:T(8,128)(2,1)}, u32[]{:S(2)}, u32[]{:S(2)}) collective-permute-start(bf16[16,2,512]{0,2,1:T(8,128)(2,1)} %collective-permute-done.7), channel_id=1, source_target_pairs={{0,28},{4,0},{8,4},{12,8},{16,12},{20,16},{24,20},{28,24},{1,29},{... | collective-permute-start | bytes 98312 | tf_op jit(solution)/shard_map/ppermute | solution.py:52
  90.7 18.8 %collective-permute-start.5 = (bf16[16,2,512]{0,2,1:T(8,128)(2,1)}, bf16[16,2,512]{0,2,1:T(8,128)(2,1)}, u32[]{:S(2)}, u32[]{:S(2)}) collective-permute-start(bf16[16,2,512]{0,2,1:T(8,128)(2,1)} %collective-permute-done.4), channel_id=1, source_target_pairs={{0,4},{4,8},{8,12},{12,16},{16,20},{20,24},{24,28},{28,0},{1,5},{5... | collective-permute-start | bytes 98312 | tf_op jit(solution)/shard_map/ppermute | solution.py:50
  101.5 8.0 %copy-start.25 = (bf16[16,2,512]{0,2,1:T(8,128)(2,1)S(1)}, bf16[16,2,512]{0,2,1:T(8,128)(2,1)}, u32[]{:S(2)}) copy-start(bf16[16,2,512]{0,2,1:T(8,128)(2,1)} %copy-done.24) | copy-start | bytes 98308
  115.0 3.5 %copy-start.26 = (bf16[4,64,4,128]{3,1,0,2:T(8,128)(2,1)S(1)}, bf16[4,64,4,128]{3,1,0,2:T(8,128)(2,1)}, u32[]{:S(2)}) copy-start(bf16[4,64,4,128]{3,1,0,2:T(8,128)(2,1)} %copy.220) | copy-start | bytes 786436
  116.2 5.2 %copy-start.22 = (bf16[128,1,512]{0,2,1:T(8,128)(2,1)}, bf16[128,1,512]{0,2,1:T(8,128)(2,1)S(1)}, u32[]{:S(2)}) copy-start(bf16[128,1,512]{0,2,1:T(8,128)(2,1)S(1)} %get-tuple-element.18) | copy-start | bytes 393220
  117.4 0.8 copy-start.3
  121.4 1.6 copy-start.31
  123.0 1.0 copy-start.17
  123.0 1.0 copy-start.19
  123.0 1.2 copy-start.21
  126.7 1.1 copy-start.1
  126.7 1.4 copy-start.4
  127.8 7.6 %copy-start.2 = (f32[4,4,384,64]{2,3,1,0:T(8,128)}, f32[4,4,384,64]{2,3,1,0:T(8,128)S(1)}, u32[]{:S(2)}) copy-start(f32[4,4,384,64]{2,3,1,0:T(8,128)S(1)} %get-tuple-element.29) | copy-start | bytes 4718596
  127.8 1.3 copy-start.12
  131.5 2.7 copy-start.5
  131.5 3.9 %copy-start.13 = (bf16[4,64,4,128]{3,2,1,0:T(4,128)(2,1)S(1)}, bf16[4,64,4,128]{3,2,1,0:T(4,128)(2,1)}, u32[]{:S(2)}) copy-start(bf16[4,64,4,128]{3,2,1,0:T(4,128)(2,1)} %copy-done.11) | copy-start | bytes 786436
  143.7 2.4 copy-start.29
  146.1 2.3 copy-start.7
  154.2 1.7 copy-start.6
  171.9 60.3 %all-to-all-start.1 = ((bf16[8,2,65536]{2,1,0:T(2,128)(2,1)}), bf16[8,2,65536]{2,1,0:T(2,128)(2,1)}, u32[]{:S(2)}, u32[]{:S(2)}) async-start(bf16[8,2,65536]{2,1,0:T(2,128)(2,1)} %reshape.224), calls=%async_computation.1 | async-start | bytes 4194304 | tf_op jit(solution)/shard_map/all_to_all | solution.py:168
  178.1 102.1 %all-reduce.2.cloned.1.call-start = ((), (), s32[]{:S(2)}) async-start(), calls=%async_computation.2 | async-start | bytes 1048576 | tf_op jit(solution)/shard_map/psum | solution.py:193
  185.9 2.9 copy-start.20
  185.9 2.9 copy-start.23
  188.7 1.2 copy-start.8
  188.8 1.2 copy-start.9
  188.8 1.2 copy-start.30
  190.2 1.0 copy-start.14
  193.0 2.5 copy-start.15
  195.5 1.2 copy-start.27
  195.5 1.2 copy-start.28
  197.6 8.5 %copy-start = (f32[4,384,1,512]{3,1,2,0:T(8,128)S(1)}, f32[4,384,1,512]{3,1,2,0:T(8,128)}, u32[]{:S(2)}) copy-start(f32[4,384,1,512]{3,1,2,0:T(8,128)} %copy.229) | copy-start | bytes 9437188
  200.9 8.8 %collective-permute-start.9 = (bf16[64,2,512]{2,0,1:T(8,128)(2,1)S(1)}, bf16[64,2,512]{2,0,1:T(8,128)(2,1)S(1)}, u32[]{:S(2)}, u32[]{:S(2)}) collective-permute-start(bf16[64,2,512]{2,0,1:T(8,128)(2,1)S(1)} %get-tuple-element.10), channel_id=1, source_target_pairs={{0,4},{4,8},{8,12},{12,16},{16,20},{20,24},{24,28},{1,5},{5,9},{9,... | collective-permute-start | bytes 393224 | tf_op jit(solution)/shard_map/ppermute | solution.py:19
  204.8 8.8 %collective-permute-start.10 = (bf16[64,2,512]{2,0,1:T(8,128)(2,1)S(1)}, bf16[64,2,512]{2,0,1:T(8,128)(2,1)S(1)}, u32[]{:S(2)}, u32[]{:S(2)}) collective-permute-start(bf16[64,2,512]{2,0,1:T(8,128)(2,1)S(1)} %get-tuple-element.11), channel_id=1, source_target_pairs={{4,0},{8,4},{12,8},{16,12},{20,16},{24,20},{28,24},{5,1},{9,5},{13... | collective-permute-start | bytes 393224 | tf_op jit(solution)/shard_map/ppermute | solution.py:20
  214.4 19.8 %copy-start.32 = (s32[16]{0:T(128)S(1)}, s32[16]{0:T(128)}, u32[]{:S(2)}) copy-start(s32[16]{0:T(128)} %sub.71) | copy-start | bytes 196
  235.8 2.4 copy-start.10
Sparse Core Ops, SparseCore 0:
  197.7 82.4 all-reduce.1
